TPU v7x, 512 devices: a whole 4x4x16 slice. The times are simulated.
512 devices in a mesh: sec: 64 (over y, z), yb: 8 (over x, core).
Axes of the slice: x: 4, y: 4, z: 16, core: 2. Of those that a mesh axis runs over, the one named last changes fastest.
Arguments:
- volume: float32 [64, 2048, 2048], P('sec', None, 'yb'), may hold values from 0 to 1
- block_ids: int32 [64, 8, 64], P('sec', 'yb'), may hold values from 0 to 127, as said below
- counts: int32 [64, 8], P('sec', 'yb'), may hold values from 1 to 64, as said below
Outputs:
- downsampled: float32 [32, 1024, 1024], P(None, 'sec', 'yb')
- coeffs: float32 [64, 8, 64, 512], P('sec', 'yb')
Inputs may be any that keep to these rules, and one draw needn't show every extreme that they name: `block_ids`: each device's first counts entries are distinct block numbers; entries at later slots are 0. `counts`: some device has all 64 slots valid.
All inputs are finite; a program needn't handle non-finite values.
Results may differ from a plain program's by a relative error of at most 0.0003.
Values sent between devices are 32-bit elements; how exact they have to be, the bound alone decides.
A program may use at most 64 MiB of HBM per device.

v0:
```python
import math

import jax
import jax.numpy as jnp
from jax import lax
from jax.sharding import PartitionSpec as P


def extended(block, sides, width):
    for axis, dim in sides:
        count = lax.axis_size(axis)
        forward = [(i, i + 1) for i in range(count - 1)]
        backward = [(target, source) for source, target in forward]
        low = lax.ppermute(
            lax.slice_in_dim(block, block.shape[dim] - width, None, axis=dim), axis, forward
        )
        high = lax.ppermute(lax.slice_in_dim(block, 0, width, axis=dim), axis, backward)
        block = jnp.concatenate([low, block, high], axis=dim)
    return block


def pairs_valid(padded, along):
    shape = list(padded.shape)
    length = shape[along]
    split = shape[:along] + [length // 2, 2] + shape[along + 1 :]
    paired = padded.reshape(split)
    evens = lax.index_in_dim(paired, 0, along + 1, keepdims=False)
    odds = lax.index_in_dim(paired, 1, along + 1, keepdims=False)
    count = length // 2 - 1
    first_even = lax.slice_in_dim(evens, 0, count, 1, along)
    first_odd = lax.slice_in_dim(odds, 0, count, 1, along)
    next_even = lax.slice_in_dim(evens, 1, count + 1, 1, along)
    next_odd = lax.slice_in_dim(odds, 1, count + 1, 1, along)
    return (first_even + 3.0 * first_odd + 3.0 * next_even + next_odd) * 0.125


def pairs_zero(values, along):
    widths = [(0, 0)] * values.ndim
    widths[along] = (1, 1)
    return pairs_valid(jnp.pad(values, widths), along)


def row_matrix(length):
    inputs = jnp.arange(length, dtype=jnp.int32)[:, None]
    outputs = jnp.arange((length - 2) // 2, dtype=jnp.int32)[None, :]
    offset = inputs - 2 * outputs
    weight = jnp.where((offset == 0) | (offset == 3), 0.125, 0.375)
    return jnp.where((offset >= 0) & (offset <= 3), weight, 0.0).astype(jnp.float32)


def rows_valid(padded):
    depth, width, length = padded.shape
    matrix = row_matrix(length)
    flat = jnp.dot(
        padded.reshape(depth * width, length),
        matrix,
        precision=lax.Precision.HIGHEST,
        preferred_element_type=jnp.float32,
    )
    return flat.reshape(depth, width, (length - 2) // 2)


def cosine_basis():
    index = jnp.arange(8, dtype=jnp.float32)
    weight = jnp.where(index == 0, math.sqrt(1.0 / 8.0), math.sqrt(2.0 / 8.0))
    return weight[:, None] * jnp.cos(math.pi * (2.0 * index[None, :] + 1.0) * index[:, None] / 16.0)


def on_device(volume, block_ids, counts):
    stacked = lax.all_to_all(volume, "sec", split_axis=1, concat_axis=0, tiled=True)
    bordered = extended(stacked, (("sec", 1), ("yb", 2)), 1)
    downsampled = rows_valid(pairs_valid(pairs_zero(bordered, 0), 1))
    depth, width, height = downsampled.shape
    per_col = width // 8
    per_row = height // 8
    blocked = (downsampled - 0.5).reshape(depth // 8, 8, per_col, 8, per_row, 8)
    slot_ids = block_ids[0, 0]
    depth_idx = slot_ids // (per_col * per_row)
    col_idx = slot_ids // per_row % per_col
    row_idx = slot_ids % per_row
    chosen = blocked[depth_idx, :, col_idx, :, row_idx, :].reshape(slot_ids.shape[0], 512)
    basis = cosine_basis()
    kernel = jnp.kron(jnp.kron(basis, basis), basis)
    spectra = jnp.dot(
        chosen, kernel.T, precision=lax.Precision.HIGHEST, preferred_element_type=jnp.float32
    )
    live = jnp.arange(slot_ids.shape[0], dtype=jnp.int32) < counts[0, 0]
    coeffs = jnp.where(live[:, None], spectra, jnp.zeros((), spectra.dtype))
    return (downsampled, coeffs[None, None])


def solution(mesh):
    placed = (P("sec", None, "yb"), P("sec", "yb", None), P("sec", "yb"))
    return jax.shard_map(
        on_device,
        mesh=mesh,
        in_specs=placed,
        out_specs=(P(None, "sec", "yb"), P("sec", "yb", None, None)),
        check_vma=False,
    )
```

profile of v0, /device:TPU:1, one launch (start us, length us, event | category | flops | bytes accessed | tf_op | source)
XLA Modules:
  0.0 191.5 jit_solution(1448558631912642425)
XLA Ops:
  0.6 4.8 %copy.27 = f32[1,2048,256]{2,0,1:T(1,128)} copy(f32[1,2048,256]{2,1,0:T(8,128)} %param.3) | data formatting | bytes 4194304 | tf_op args[0]
  5.4 19.7 %all-to-all-start = ((f32[1,2048,256]{2,0,1:T(1,128)}), f32[1,2048,256]{2,0,1:T(1,128)}, u32[]{:S(2)}, u32[]{:S(2)}) async-start(f32[1,2048,256]{2,0,1:T(1,128)} %copy.27), calls=%async_computation | async-start | bytes 4194304 | tf_op jit(solution)/shard_map/all_to_all | solution.py:70
  26.1 7.9 %broadcast_multiply_fusion = f32[64,8,64,8]{3,2,1,0:T(8,128)} fusion(f32[8,8]{1,0:T(8,128)S(1)} %cosine_multiply_fusion, f32[64,64]{1,0:T(8,128)S(1)} %mul.170), kind=kLoop, calls=%fused_computation.1 | loop fusion | flops 262144 | bytes 1065216 | tf_op jit(solution)/shard_map/jit(kron)/mul | solution.py:83
  34.1 85.7 %all-to-all-done = f32[1,2048,256]{2,0,1:T(1,128)} async-done(((f32[1,2048,256]{2,0,1:T(1,128)}), f32[1,2048,256]{2,0,1:T(1,128)}, u32[]{:S(2)}, u32[]{:S(2)}) %all-to-all-start) | async-done | bytes 2097184 | tf_op jit(solution)/shard_map/all_to_all | solution.py:70
  119.8 1.7 copy.41
  121.6 1.3 collective-permute-start.1
  122.9 5.6 %collective-permute-start = (f32[64,1,256]{2,1,0:T(1,128)S(1)}, f32[64,1,256]{2,1,0:T(1,128)S(1)}, u32[]{:S(2)}, u32[]{:S(2)}) collective-permute-start(f32[64,1,256]{2,1,0:T(1,128)S(1)} %get-tuple-element.14), channel_id=1, source_target_pairs={{0,8},{8,16},{16,24},{24,32},{32,40},{40,48},{48,56},{56,64},{64,7... | collective-permute-start | bytes 196616 | tf_op jit(solution)/shard_map/ppermute | solution.py:14
  128.5 1.3 collective-permute-done
  130.2 1.5 fusion.51
  131.7 2.3 %copy.29 = f32[64,34,1]{0,2,1:T(1,128)} copy(f32[64,34,1]{2,1,0:T(8,128)} %get-tuple-element.13) | data formatting | bytes 17408 | tf_op jit(solution)/shard_map/slice | solution.py:17
  134.0 5.5 %collective-permute-start.3 = (f32[64,34,1]{0,2,1:T(1,128)}, f32[64,34,1]{0,2,1:T(1,128)}, u32[]{:S(2)}, u32[]{:S(2)}) collective-permute-start(f32[64,34,1]{0,2,1:T(1,128)} %copy.29), channel_id=1, source_target_pairs={{1,0},{2,1},{3,2},{4,3},{5,4},{6,5},{7,6},{9,8},{10,9},{11,10},{12... | collective-permute-start | bytes 26120 | tf_op jit(solution)/shard_map/ppermute | solution.py:17
  139.5 1.0 copy.28
  140.5 3.2 %collective-permute-start.2 = (f32[64,34,1]{0,2,1:T(1,128)}, f32[64,34,1]{0,2,1:T(1,128)}, u32[]{:S(2)}, u32[]{:S(2)}) collective-permute-start(f32[64,34,1]{0,2,1:T(1,128)} %copy.28), channel_id=1, source_target_pairs={{0,1},{1,2},{2,3},{3,4},{4,5},{5,6},{6,7},{8,9},{9,10},{10,11},{11... | collective-permute-start | bytes 26120 | tf_op jit(solution)/shard_map/ppermute | solution.py:14
  143.7 13.4 %mul.174 = f32[512,512]{1,0:T(8,128)} reshape(f32[64,8,64,8]{3,2,1,0:T(8,128)} %broadcast_multiply_fusion) | data formatting | bytes 2097152 | tf_op jit(solution)/shard_map/jit(kron)/mul | solution.py:83
  157.2 1.2 copy.31
  158.4 2.3 %copy.30 = f32[64,34,1]{2,1,0:T(8,128)} copy(f32[64,34,1]{0,2,1:T(1,128)} %collective-permute-done.2) | data formatting | bytes 17408 | tf_op jit(solution)/shard_map/ppermute | solution.py:14
  160.7 4.4 %select_maximum_fusion = f32[66,34,258]{2,1,0:T(8,128)S(1)} fusion(f32[64,34,1]{2,1,0:T(8,128)S(1)} %copy.31, f32[64,34,1]{2,1,0:T(8,128)} %copy.30, f32[64,1,256]{2,1,0:T(1,128)S(1)} %collective-permute-done.1, f32[64,32,256]{2,1,0:T(8,128)S(1)} %bitcast.50, f32[64,1,256]{2,1,0:T(1,128)S(1)} %collective-permute-done), kind=kLoop, calls=%fused_computation.4 | loop fusion | flops 6947424 | bytes 4561440 | tf_op jit(solution)/shard_map/concatenate | solution.py:18
  165.6 7.6 %fusion.1 = f32[32,1,34,258]{3,1,0,2:T(1,128)S(1)} fusion(f32[32,1,34,258]{3,2,1,0:T(8,128)S(1)} %get-tuple-element.11, f32[32,1,34,258]{3,2,1,0:T(8,128)S(1)} %get-tuple-element.9, f32[32,1,34,258]{3,2,1,0:T(8,128)S(1)} %get-tuple-element.10, f32[32,1,34,258]{3,2,1,0:T(8,128)S(1)} %get-tuple-element.8), kind=kLoop, calls=%fused_computation.11 | loop fusion | flops 1684224 | bytes 5614080 | tf_op jit(solution)/shard_map/mul | solution.py:34
  173.4 0.9 broadcast_add_fusion
  175.2 3.6 %reshape.376 = f32[4,8,2,8,16,8]{5,4,1,0,3,2:T(8,128)} reshape(f32[32,16,128]{2,0,1:T(8,128)S(1)} %get-tuple-element.18) | data formatting | bytes 524288 | tf_op jit(solution)/shard_map/reshape | solution.py:76
  178.8 6.6 %copy.35 = f32[4,8,2,8,16,8]{5,3,4,2,1,0:T(8,128)} copy(f32[4,8,2,8,16,8]{5,4,1,0,3,2:T(8,128)} %reshape.376) | data formatting | bytes 524288 | tf_op jit(solution)/shard_map/reshape | solution.py:76
  185.4 3.0 %gather_fusion = f32[64,8,8,8]{3,2,1,0:T(8,128)S(1)} fusion(f32[4,8,2,8,16,8]{5,3,4,2,1,0:T(8,128)} %copy.35, s32[64]{0:T(128)S(1)} %fusion.43), kind=kCustom, calls=%fused_computation | custom fusion | bytes 262912 | tf_op jit(solution)/shard_map/gather | solution.py:81
  188.5 1.1 copy.36
  189.7 1.8 fusion.4
  (20 shorter events, 2.6 us)
Async XLA Ops:
  5.4 20.6 %copy-start.1 = (s32[1,1,64]{2,1,0:T(1,128)S(1)}, s32[1,1,64]{2,1,0:T(1,128)}, u32[]{:S(2)}) copy-start(s32[1,1,64]{2,1,0:T(1,128)} %param.4) | copy-start | bytes 772
  5.4 114.4 %all-to-all-start = ((f32[1,2048,256]{2,0,1:T(1,128)}), f32[1,2048,256]{2,0,1:T(1,128)}, u32[]{:S(2)}, u32[]{:S(2)}) async-start(f32[1,2048,256]{2,0,1:T(1,128)} %copy.27), calls=%async_computation | async-start | bytes 4194304 | tf_op jit(solution)/shard_map/all_to_all | solution.py:70
  121.6 6.9 %collective-permute-start.1 = (f32[64,1,256]{2,1,0:T(1,128)S(1)}, f32[64,1,256]{2,1,0:T(1,128)S(1)}, u32[]{:S(2)}, u32[]{:S(2)}) collective-permute-start(f32[64,1,256]{2,1,0:T(1,128)S(1)} %get-tuple-element.15), channel_id=1, source_target_pairs={{8,0},{16,8},{24,16},{32,24},{40,32},{48,40},{56,48},{64,56},{72,6... | collective-permute-start | bytes 196616 | tf_op jit(solution)/shard_map/ppermute | solution.py:17
  122.9 6.9 %collective-permute-start = (f32[64,1,256]{2,1,0:T(1,128)S(1)}, f32[64,1,256]{2,1,0:T(1,128)S(1)}, u32[]{:S(2)}, u32[]{:S(2)}) collective-permute-start(f32[64,1,256]{2,1,0:T(1,128)S(1)} %get-tuple-element.14), channel_id=1, source_target_pairs={{0,8},{8,16},{16,24},{24,32},{32,40},{40,48},{48,56},{56,64},{64,7... | collective-permute-start | bytes 196616 | tf_op jit(solution)/shard_map/ppermute | solution.py:14
  134.0 23.1 %collective-permute-start.3 = (f32[64,34,1]{0,2,1:T(1,128)}, f32[64,34,1]{0,2,1:T(1,128)}, u32[]{:S(2)}, u32[]{:S(2)}) collective-permute-start(f32[64,34,1]{0,2,1:T(1,128)} %copy.29), channel_id=1, source_target_pairs={{1,0},{2,1},{3,2},{4,3},{5,4},{6,5},{7,6},{9,8},{10,9},{11,10},{12... | collective-permute-start | bytes 26120 | tf_op jit(solution)/shard_map/ppermute | solution.py:17
  140.5 17.9 %collective-permute-start.2 = (f32[64,34,1]{0,2,1:T(1,128)}, f32[64,34,1]{0,2,1:T(1,128)}, u32[]{:S(2)}, u32[]{:S(2)}) collective-permute-start(f32[64,34,1]{0,2,1:T(1,128)} %copy.28), channel_id=1, source_target_pairs={{0,1},{1,2},{2,3},{3,4},{4,5},{5,6},{6,7},{8,9},{9,10},{10,11},{11... | collective-permute-start | bytes 26120 | tf_op jit(solution)/shard_map/ppermute | solution.py:14
  188.5 1.2 copy-start
where the time goes:
time: 194 us; the launch traced here: 192 us
  waiting for transfers between devices  87 us (45%)
  local copies, waits for them, and re-layouts  44.5 us (23%)
  starting transfers between devices  35.2 us (18%)
  other arithmetic  20.6 us (11%)
  matrix products  2.77 us (1%)
    all_to_all x1, waiting for transfers between devices, on_device(): lax.all_to_all(volume, 'sec', split_axis=1, concat_axis=0, tiled=True)  85.7 us
    all_to_all x1, starting transfers between devices, on_device(): lax.all_to_all(volume, 'sec', split_axis=1, concat_axis=0, tiled=True)  19.7 us
    mul x2, local copies, waits for them, and re-layouts, on_device(): kernel = jnp.kron(jnp.kron(basis, basis), basis)  13.6 us
    reshape x2, local copies, waits for them, and re-layouts, on_device(): blocked = (downsampled - 0.5).reshape(depth // 8, 8, per_col, 8, per_row, 8)  10.2 us
    ppermute x2, starting transfers between devices, extended(): lax.ppermute(lax.slice_in_dim(block, block.shape[dim] - width, None, axis...  8.75 us
    mul x2, other arithmetic, on_device(): kernel = jnp.kron(jnp.kron(basis, basis), basis)  8.04 us
    unnamed x8, local copies, waits for them, and re-layouts  7.62 us
    mul x1, other arithmetic, pairs_valid(): return (first_even + 3.0 * first_odd + 3.0 * next_even + next_odd) * 0.125  7.57 us
  transfers between devices with their start and end apart: 5, of which 2 were waited for; matrix products, arithmetic and copies ran while one was open for 12% of the time, Pallas kernels for 0%

commit v1 on v0

v1 whole, which is shorter than its diff:
```python
import functools
import math

import jax
import jax.numpy as jnp
import numpy as np
from jax import lax
from jax.experimental import pallas as pl
from jax.experimental.pallas import tpu as pltpu
from jax.sharding import PartitionSpec as P

F32 = jnp.float32
BF16 = jnp.bfloat16
MESH = pl.DeviceIdType.MESH
NY, NZ = 4, 16
N_SEC = NY * NZ
N_YB = 8
COLS = 2048
ROWS = 256
HALF = 128
OUT_COLS = 16
DEPTH = 32
CHUNKS = 8
PAD = 8
SELF_STEP = N_SEC - NY


def cosine_matrix():
    index = np.arange(8, dtype=np.float64)
    weight = np.where(index == 0, math.sqrt(1.0 / 8.0), math.sqrt(2.0 / 8.0))
    basis = weight[:, None] * np.cos(math.pi * (2.0 * index[None, :] + 1.0) * index[:, None] / 16.0)
    return np.einsum("ua,vb,wc->cabuvw", basis, basis, basis).reshape(512, 512).astype(np.float32)


def row_matrix(half):
    inputs = lax.broadcasted_iota(jnp.int32, (HALF, HALF), 0) + half * HALF
    outputs = lax.broadcasted_iota(jnp.int32, (HALF, HALF), 1)
    offset = inputs - (2 * outputs - 1)
    weight = jnp.where((offset == 0) | (offset == 3), 0.125, 0.375)
    return jnp.where((offset >= 0) & (offset <= 3), weight, 0.0).astype(BF16)


def pieces(value):
    high = value.astype(BF16)
    rest = value - high.astype(F32)
    mid = rest.astype(BF16)
    return high, mid, (rest - mid.astype(F32)).astype(BF16)


def kernel(
    x_hbm, ids_ref, cnt_ref, k_hbm, ds_ref, co_ref,
    xbuf, plane, stacked, k_full, k_ref, turned, edge_out, edge_in,
    x_sem, k_sem, send_sem, recv_sem, edge_send, edge_recv,
):
    me = lax.axis_index("sec")
    band = lax.axis_index("yb")
    y, z = me // NZ, me % NZ
    size = COLS // CHUNKS
    out_size = size // 2

    def load(chunk, half):
        return pltpu.make_async_copy(
            x_hbm.at[pl.ds(chunk * size, size), pl.ds(half * HALF, HALF)],
            xbuf.at[half, pl.ds(PAD + chunk * size, size), :],
            x_sem.at[chunk, half],
        )

    edge_in[...] = jnp.zeros(edge_in.shape, F32)
    for chunk in range(CHUNKS):
        for half in range(2):
            load(chunk, half).start()
    basis_copy = pltpu.make_async_copy(k_hbm, k_full, k_sem)
    basis_copy.start()

    def peer(step):
        dy, turn = step % NY, step // NY
        hop = turn // 2
        dz = jnp.where(turn % 2 == 0, NZ // 2 - hop, hop - (NZ // 2 - 1))
        return ((y + dy) % NY) * NZ + (z + dz + NZ) % NZ

    def source(step):
        dy, turn = step % NY, step // NY
        hop = turn // 2
        dz = jnp.where(turn % 2 == 0, NZ // 2 - hop, hop - (NZ // 2 - 1))
        return ((y - dy + NY) % NY) * NZ + (z - dz + NZ) % NZ

    barrier = pltpu.get_barrier_semaphore()

    def greet(step, carry):
        pl.semaphore_signal(barrier, inc=1, device_id=(peer(step), band), device_id_type=MESH)
        return carry

    lax.fori_loop(0, SELF_STEP, greet, 0)
    lax.fori_loop(SELF_STEP + 1, N_SEC, greet, 0)

    @pl.when(band > 0)
    def _():
        pl.semaphore_signal(barrier, inc=1, device_id=(me, band - 1), device_id_type=MESH)

    @pl.when(band < N_YB - 1)
    def _():
        pl.semaphore_signal(barrier, inc=1, device_id=(me, band + 1), device_id_type=MESH)

    for half in range(2):
        xbuf[half, pl.ds(0, PAD), :] = jnp.zeros((PAD, HALF), F32)
        xbuf[half, pl.ds(PAD + COLS, PAD), :] = jnp.zeros((PAD, HALF), F32)

    lane = lax.broadcasted_iota(jnp.int32, (8, HALF), 1)
    row_weights = [row_matrix(half) for half in range(2)]
    first_row = jnp.zeros((8, HALF), F32)
    last_row = jnp.zeros((8, HALF), F32)
    for half in range(2):
        load(0, half).wait()
    for chunk in range(CHUNKS):
        if chunk + 1 < CHUNKS:
            for half in range(2):
                load(chunk + 1, half).wait()
        total = jnp.zeros((out_size, HALF), F32)
        for half in range(2):
            start = PAD + chunk * size - 1
            taps = [xbuf[half, pl.ds(start + a, out_size, stride=2), :] for a in range(4)]
            narrow = (taps[0] + taps[3] + 3.0 * (taps[1] + taps[2])) * 0.125
            for part in pieces(narrow):
                total += jnp.dot(
                    part, row_weights[half], preferred_element_type=F32
                )
            for inner in range(out_size // 8):
                group = chunk * (out_size // 8) + inner
                rows = narrow[inner * 8 : inner * 8 + 8, :]
                if half == 0:
                    moved = rows if group == 0 else pltpu.roll(rows, group, 1)
                    first_row = jnp.where(lane == group, moved, first_row)
                else:
                    shift = (group + 1) % HALF
                    moved = rows if shift == 0 else pltpu.roll(rows, shift, 1)
                    last_row = jnp.where(lane == group, moved, last_row)
        per = out_size // OUT_COLS
        plane[pl.ds(chunk * per, per)] = total.reshape(per, OUT_COLS, HALF)
    edge_out[0] = first_row * 0.125
    edge_out[1] = last_row * 0.125

    inside = (band > 0).astype(jnp.int32) + (band < N_YB - 1).astype(jnp.int32)
    pl.semaphore_wait(barrier, N_SEC - 1 + inside)

    def edge_copy(which, target):
        return pltpu.make_async_remote_copy(
            src_ref=edge_out.at[which],
            dst_ref=edge_in.at[which],
            send_sem=edge_send.at[which],
            recv_sem=edge_recv.at[which],
            device_id=(me, target),
            device_id_type=MESH,
        )

    @pl.when(band > 0)
    def _():
        edge_copy(0, band - 1).start()

    @pl.when(band < N_YB - 1)
    def _():
        edge_copy(1, band + 1).start()

    @pl.when(band < N_YB - 1)
    def _():
        edge_copy(0, band + 1).wait_recv()

    @pl.when(band > 0)
    def _():
        edge_copy(1, band - 1).wait_recv()

    above, below = edge_in[0], edge_in[1]

    def finished(target):
        parts = []
        for sub in range(2):
            group = 2 * target + sub
            low = pltpu.roll(below, (HALF - group) % HALF, 1)
            high = pltpu.roll(above, (2 * HALF - 1 - group) % HALF, 1)
            rows = plane[target, pl.ds(sub * 8, 8), :]
            parts.append(
                rows + jnp.where(lane == 0, low, 0.0) + jnp.where(lane == HALF - 1, high, 0.0)
            )
        return parts

    def chunk_copy(target, slot):
        return pltpu.make_async_remote_copy(
            src_ref=plane.at[target],
            dst_ref=stacked.at[slot],
            send_sem=send_sem,
            recv_sem=recv_sem.at[slot],
            device_id=(target, band),
            device_id_type=MESH,
        )

    def send(step, carry):
        target = peer(step)
        for sub, rows in enumerate(finished(target)):
            plane[target, pl.ds(sub * 8, 8), :] = rows
        chunk_copy(target, me).start()
        return carry

    lax.fori_loop(0, SELF_STEP, send, 0)
    lax.fori_loop(SELF_STEP + 1, N_SEC, send, 0)
    for sub, rows in enumerate(finished(me)):
        stacked[me, pl.ds(sub * 8, 8), :] = rows
    basis_copy.wait()
    k_ref[0] = k_full[...].astype(BF16)
    k_ref[1] = (k_full[...] - k_ref[0].astype(F32)).astype(BF16)

    def receive(step, carry):
        origin = source(step)
        chunk_copy(origin, origin).wait_recv()
        return carry

    lax.fori_loop(0, SELF_STEP, receive, 0)
    lax.fori_loop(SELF_STEP + 1, N_SEC, receive, 0)

    for bz in range(DEPTH // 8):
        for k in range(8 * bz, 8 * bz + 8):
            value = 3.0 * (stacked[2 * k] + stacked[2 * k + 1])
            if k > 0:
                value += stacked[2 * k - 1]
            if k < DEPTH - 1:
                value += stacked[2 * k + 2]
            ds_ref[k] = value * 0.125
        group = ds_ref[pl.ds(8 * bz, 8)] - 0.5
        flat = jnp.concatenate(
            [group[:, 0:8, :].reshape(64, HALF), group[:, 8:16, :].reshape(64, HALF)], axis=0
        )
        turned[bz] = flat.T

    wide = lax.broadcasted_iota(jnp.int32, (16, HALF), 1)
    tiles = []
    for pair in range(4):
        rows = []
        for bz in range(DEPTH // 8):
            even = turned[bz, pl.ds(2 * pair, 16, stride=8), :]
            odd = turned[bz, pl.ds(2 * pair + 1, 16, stride=8), :]
            rows.append(jnp.where(wide < 64, even, pltpu.roll(odd, 64, 1)))
            rows.append(jnp.where(wide < 64, pltpu.roll(even, 64, 1), odd))
        tiles.append(jnp.concatenate(rows, axis=0))
    blocks = jnp.concatenate(tiles, axis=1)
    high = blocks.astype(BF16)
    low = (blocks - high.astype(F32)).astype(BF16)
    number = lax.broadcasted_iota(jnp.int32, (HALF, 64), 0)
    slot = lax.broadcasted_iota(jnp.int32, (HALF, 64), 1)
    chosen = (number == ids_ref[...]) & (slot < cnt_ref[0, 0])
    chosen = jnp.where(chosen, 1.0, 0.0).T.astype(BF16)
    high = jnp.dot(chosen, high, preferred_element_type=F32).astype(BF16)
    low = jnp.dot(chosen, low, preferred_element_type=F32).astype(BF16)
    co_ref[...] = (
        jnp.dot(high, k_ref[0], preferred_element_type=F32)
        + jnp.dot(low, k_ref[0], preferred_element_type=F32)
        + jnp.dot(high, k_ref[1], preferred_element_type=F32)
    )

    pltpu.make_async_remote_copy(
        src_ref=plane.at[pl.ds(0, N_SEC - 1)],
        dst_ref=stacked.at[pl.ds(0, N_SEC - 1)],
        send_sem=send_sem,
        recv_sem=recv_sem.at[0],
        device_id=(peer(0), band),
        device_id_type=MESH,
    ).wait_send()

    @pl.when(band > 0)
    def _():
        edge_copy(0, band - 1).wait_send()

    @pl.when(band < N_YB - 1)
    def _():
        edge_copy(1, band + 1).wait_send()


def on_device(volume, block_ids, counts):
    section = volume.reshape(COLS, ROWS)
    vmem = pl.BlockSpec(memory_space=pltpu.VMEM)
    hbm = pl.BlockSpec(memory_space=pl.ANY)
    downsampled, coeffs = pl.pallas_call(
        kernel,
        out_shape=(
            jax.ShapeDtypeStruct((DEPTH, OUT_COLS, HALF), F32),
            jax.ShapeDtypeStruct((64, 512), F32),
        ),
        in_specs=[hbm, vmem, pl.BlockSpec(memory_space=pltpu.SMEM), hbm],
        out_specs=(vmem, vmem),
        scratch_shapes=[
            pltpu.VMEM((2, COLS + 2 * PAD, HALF), F32),
            pltpu.VMEM((N_SEC, OUT_COLS, HALF), F32),
            pltpu.VMEM((N_SEC, OUT_COLS, HALF), F32),
            pltpu.VMEM((512, 512), F32),
            pltpu.VMEM((2, 512, 512), BF16),
            pltpu.VMEM((4, HALF, HALF), F32),
            pltpu.VMEM((2, 8, HALF), F32),
            pltpu.VMEM((2, 8, HALF), F32),
            pltpu.SemaphoreType.DMA((CHUNKS, 2)),
            pltpu.SemaphoreType.DMA,
            pltpu.SemaphoreType.DMA,
            pltpu.SemaphoreType.DMA((N_SEC,)),
            pltpu.SemaphoreType.DMA((2,)),
            pltpu.SemaphoreType.DMA((2,)),
        ],
        compiler_params=pltpu.CompilerParams(
            collective_id=0, has_side_effects=True, vmem_limit_bytes=60 * 1024 * 1024
        ),
    )(section, block_ids.reshape(1, 64), counts, jnp.asarray(cosine_matrix()))
    return downsampled, coeffs.reshape(1, 1, 64, 512)


def solution(mesh):
    placed = (P("sec", None, "yb"), P("sec", "yb", None), P("sec", "yb"))
    return jax.shard_map(
        on_device,
        mesh=mesh,
        in_specs=placed,
        out_specs=(P(None, "sec", "yb"), P("sec", "yb", None, None)),
        check_vma=False,
    )
```

time: 194 us -> 52 us (0.27); the launches traced: 192 us -> 51.8 us
  waiting for transfers between devices: 87 us -> 0 us
  Pallas kernels: 0 us -> 47.3 us
  local copies, waits for them, and re-layouts: 44.5 us -> 3.24 us
  starting transfers between devices: 35.2 us -> 0 us
  other arithmetic: 20.6 us -> 0 us
  matrix products: 2.77 us -> 0 us
    all_to_all x1 -> x0, waiting for transfers between devices: 85.7 us -> none  [on_device(): lax.all_to_all(volume, 'sec', split_axis=1, concat_axis=0, tiled=True)]
    pallas_call x0 -> x1, Pallas kernels: none -> 47.3 us  [on_device(): pl.pallas_call(kernel, out_shape=(jax.ShapeDtypeStruct((DEPTH, OUT_COLS,...]
    all_to_all x1 -> x0, starting transfers between devices: 19.7 us -> none  [on_device(): lax.all_to_all(volume, 'sec', split_axis=1, concat_axis=0, tiled=True)]
    mul x5 -> x0, other arithmetic: 15.7 us -> none  [the longest x2 8.04 us: on_device(): kernel = jnp.kron(jnp.kron(basis, basis), basis)]
    ppermute x4 -> x0, starting transfers between devices: 15.5 us -> none  [the longest x2 8.75 us: extended(): lax.ppermute(lax.slice_in_dim(block, block.shape[dim] - width, None, axis...]
    mul x2 -> x0, local copies, waits for them, and re-layouts: 13.6 us -> none  [on_device(): kernel = jnp.kron(jnp.kron(basis, basis), basis)]
    reshape x2 -> x0, local copies, waits for them, and re-layouts: 10.2 us -> none  [on_device(): blocked = (downsampled - 0.5).reshape(depth // 8, 8, per_col, 8, per_row, 8)]
    slice x5 -> x0, local copies, waits for them, and re-layouts: 5.41 us -> none  [the longest x3 2.59 us: extended(): lax.slice_in_dim(block, block.shape[dim] - width, None, axis=dim)]
  transfers between devices with their start and end apart: 5 -> 0, of which waited for: 2 -> 0; matrix products, arithmetic and copies ran while one was open for 12% -> 0% of each run, Pallas kernels for 0% -> 0%
where the time goes in v1:
time: 52 us; the launch traced here: 51.8 us
  Pallas kernels  47.3 us (91%)
  local copies, waits for them, and re-layouts  3.24 us (6%)
  between operations  1.28 us (2%)
    pallas_call x1, Pallas kernels, on_device(): pl.pallas_call(kernel, out_shape=(jax.ShapeDtypeStruct((DEPTH, OUT_COLS,...  47.3 us
    unnamed x2, local copies, waits for them, and re-layouts  3.24 us

profile of v1, /device:TPU:1, one launch (start us, length us, event | category | flops | bytes accessed | tf_op | source)
XLA Modules:
  0.0 51.8 jit_solution(10405329518809098545)
XLA Ops:
  1.3 47.3 %shard_map.59 = (f32[32,16,128]{2,1,0:T(8,128)}, f32[64,512]{1,0:T(8,128)}) custom-call(f32[2048,256]{1,0:T(8,128)} %bitcast.3, s32[1,64]{1,0:T(1,128)} %bitcast.5, s32[1,1]{1,0:T(1,128)S(6)} %copy.8.cnt_ref, f32[512,512]{1,0:T(8,128)} %constant.2.clone.k_hbm), custom_call_target="tpu_custom_call" | custom-call | tf_op jit(solution)/shard_map/pallas_call | solution.py:279
  48.6 1.7 %copy.9 = f32[32,16,128]{2,1,0:T(8,128)} copy(f32[32,16,128]{2,1,0:T(8,128)} %get-tuple-element.8) | data formatting | bytes 524288
  50.3 1.6 %copy.10 = f32[1,1,64,512]{3,2,1,0:T(8,128)} copy(f32[1,1,64,512]{3,2,1,0:T(8,128)} %bitcast.4) | data formatting | bytes 262144

commit v2 on v1

--- a/solution.py
+++ b/solution.py
@@ -22,7 +22,10 @@
 DEPTH = 32
 CHUNKS = 8
 PAD = 8
-SELF_STEP = N_SEC - NY
+GROUP_Z = NZ // 2
+WINDOW = 2
+OWN_ROUND = 3
+OWN_ROUNDS = 4
 
 
 def cosine_matrix():
@@ -50,7 +53,7 @@
 def kernel(
     x_hbm, ids_ref, cnt_ref, k_hbm, ds_ref, co_ref,
     xbuf, plane, stacked, k_full, k_ref, turned, edge_out, edge_in,
-    x_sem, k_sem, send_sem, recv_sem, edge_send, edge_recv,
+    x_sem, k_sem, send_sem, recv_sem, edge_send, edge_recv, late_sem, up_sem, down_sem,
 ):
     me = lax.axis_index("sec")
     band = lax.axis_index("yb")
@@ -72,34 +75,44 @@
     basis_copy = pltpu.make_async_copy(k_hbm, k_full, k_sem)
     basis_copy.start()
 
-    def peer(step):
-        dy, turn = step % NY, step // NY
-        hop = turn // 2
-        dz = jnp.where(turn % 2 == 0, NZ // 2 - hop, hop - (NZ // 2 - 1))
-        return ((y + dy) % NY) * NZ + (z + dz + NZ) % NZ
-
-    def source(step):
-        dy, turn = step % NY, step // NY
-        hop = turn // 2
-        dz = jnp.where(turn % 2 == 0, NZ // 2 - hop, hop - (NZ // 2 - 1))
-        return ((y - dy + NY) % NY) * NZ + (z - dz + NZ) % NZ
+    late = z >= GROUP_Z
+
+    def signal(semaphore, column, row):
+        pl.semaphore_signal(semaphore, inc=1, device_id=(column, row), device_id_type=MESH)
+
+    def visit_group(visit, own):
+        def step(index, carry):
+            turn, dy = index // NY, index % NY
+            hop = turn // 2
+            dz = jnp.where(turn % 2 == 0, NZ // 2 - hop, hop - (NZ // 2 - 1))
+            target = (z + dz + NZ) % NZ
+            same = (target >= GROUP_Z) == late
+
+            @pl.when(same if own else jnp.logical_not(same))
+            def _():
+                visit(((y + dy) % NY) * NZ + target)
+
+            return carry
+
+        lax.fori_loop(0, NY * (NZ - 1), step, 0)
+        if own:
+            for dy in range(1, NY):
+                visit(((y + dy) % NY) * NZ + z)
 
     barrier = pltpu.get_barrier_semaphore()
 
-    def greet(step, carry):
-        pl.semaphore_signal(barrier, inc=1, device_id=(peer(step), band), device_id_type=MESH)
-        return carry
-
-    lax.fori_loop(0, SELF_STEP, greet, 0)
-    lax.fori_loop(SELF_STEP + 1, N_SEC, greet, 0)
-
     @pl.when(band > 0)
     def _():
-        pl.semaphore_signal(barrier, inc=1, device_id=(me, band - 1), device_id_type=MESH)
+        signal(barrier, me, band - 1)
 
     @pl.when(band < N_YB - 1)
     def _():
-        pl.semaphore_signal(barrier, inc=1, device_id=(me, band + 1), device_id_type=MESH)
+        signal(barrier, me, band + 1)
+
+    @pl.when(jnp.logical_not(late))
+    def _():
+        visit_group(lambda column: signal(barrier, column, band), False)
+        visit_group(lambda column: signal(barrier, column, band), True)
 
     for half in range(2):
         xbuf[half, pl.ds(0, PAD), :] = jnp.zeros((PAD, HALF), F32)
@@ -140,7 +153,7 @@
     edge_out[1] = last_row * 0.125
 
     inside = (band > 0).astype(jnp.int32) + (band < N_YB - 1).astype(jnp.int32)
-    pl.semaphore_wait(barrier, N_SEC - 1 + inside)
+    pl.semaphore_wait(barrier, NY * GROUP_Z - 1 + inside + late.astype(jnp.int32))
 
     def edge_copy(which, target):
         return pltpu.make_async_remote_copy(
@@ -160,6 +173,10 @@
     def _():
         edge_copy(1, band + 1).start()
 
+    @pl.when(late)
+    def _():
+        visit_group(lambda column: signal(late_sem, column, band), False)
+
     @pl.when(band < N_YB - 1)
     def _():
         edge_copy(0, band + 1).wait_recv()
@@ -170,50 +187,108 @@
 
     above, below = edge_in[0], edge_in[1]
 
-    def finished(target):
-        parts = []
-        for sub in range(2):
-            group = 2 * target + sub
-            low = pltpu.roll(below, (HALF - group) % HALF, 1)
-            high = pltpu.roll(above, (2 * HALF - 1 - group) % HALF, 1)
-            rows = plane[target, pl.ds(sub * 8, 8), :]
-            parts.append(
-                rows + jnp.where(lane == 0, low, 0.0) + jnp.where(lane == HALF - 1, high, 0.0)
-            )
-        return parts
-
-    def chunk_copy(target, slot):
+    for group in range(COLS // 16):
+        low = below if group == 0 else pltpu.roll(below, HALF - group, 1)
+        high = above if group == HALF - 1 else pltpu.roll(above, HALF - 1 - group, 1)
+        rows = pl.ds(group % 2 * 8, 8)
+        plane[group // 2, rows, :] += jnp.where(lane == 0, low, 0.0) + jnp.where(
+            lane == HALF - 1, high, 0.0
+        )
+
+    def chunk_copy(target, slot, semaphore=send_sem):
         return pltpu.make_async_remote_copy(
             src_ref=plane.at[target],
             dst_ref=stacked.at[slot],
-            send_sem=send_sem,
+            send_sem=semaphore,
             recv_sem=recv_sem.at[slot],
             device_id=(target, band),
             device_id_type=MESH,
         )
 
-    def send(step, carry):
-        target = peer(step)
-        for sub, rows in enumerate(finished(target)):
-            plane[target, pl.ds(sub * 8, 8), :] = rows
+    def send(target):
         chunk_copy(target, me).start()
+
+    stacked[me] = plane[me]
+
+    def sent(semaphore, count):
+        pltpu.make_async_remote_copy(
+            src_ref=plane.at[pl.ds(0, count)],
+            dst_ref=stacked.at[pl.ds(0, count)],
+            send_sem=semaphore,
+            recv_sem=recv_sem.at[0],
+            device_id=((me + 1) % N_SEC, band),
+            device_id_type=MESH,
+        ).wait_send()
+
+    place = z - GROUP_Z
+
+    def sent_round(index):
+        @pl.when(index < place)
+        def _():
+            sent(up_sem.at[index], NY)
+
+        @pl.when(index + place < GROUP_Z)
+        def _():
+            sent(down_sem.at[index], NY)
+
+    def send_round(index, carry):
+        @pl.when(index >= WINDOW)
+        def _():
+            sent_round(index - WINDOW)
+
+        for dy in range(NY):
+            column = ((y + dy) % NY) * NZ
+
+            @pl.when(index < place)
+            def _():
+                chunk_copy(column + index, me, up_sem.at[index]).start()
+
+            @pl.when(index + place < GROUP_Z)
+            def _():
+                chunk_copy(column + place + index, me, down_sem.at[index]).start()
+
+        @pl.when(index == OWN_ROUND)
+        def _():
+            pl.semaphore_wait(late_sem, 1)
+
+        @pl.when((index >= OWN_ROUND) & (index < OWN_ROUND + OWN_ROUNDS))
+        def _():
+            for half in range(GROUP_Z // OWN_ROUNDS):
+                turn = (index - OWN_ROUND) * (GROUP_Z // OWN_ROUNDS) + half
+                target = GROUP_Z + (place + turn) % GROUP_Z
+
+                @pl.when(turn > 0)
+                def _():
+                    send(y * NZ + target)
+
+                for dy in range(1, NY):
+                    send(((y + dy) % NY) * NZ + target)
+
         return carry
 
-    lax.fori_loop(0, SELF_STEP, send, 0)
-    lax.fori_loop(SELF_STEP + 1, N_SEC, send, 0)
-    for sub, rows in enumerate(finished(me)):
-        stacked[me, pl.ds(sub * 8, 8), :] = rows
+    @pl.when(late)
+    def _():
+        lax.fori_loop(0, GROUP_Z, send_round, 0)
+        for index in range(GROUP_Z - WINDOW, GROUP_Z):
+            sent_round(index)
+
+    @pl.when(jnp.logical_not(late))
+    def _():
+        visit_group(send, True)
+        pl.semaphore_wait(late_sem, NY * GROUP_Z)
+        signal(late_sem, me + GROUP_Z, band)
+        visit_group(send, False)
+
     basis_copy.wait()
     k_ref[0] = k_full[...].astype(BF16)
     k_ref[1] = (k_full[...] - k_ref[0].astype(F32)).astype(BF16)
 
     def receive(step, carry):
-        origin = source(step)
+        origin = (me + step) % N_SEC
         chunk_copy(origin, origin).wait_recv()
         return carry
 
-    lax.fori_loop(0, SELF_STEP, receive, 0)
-    lax.fori_loop(SELF_STEP + 1, N_SEC, receive, 0)
+    lax.fori_loop(1, N_SEC, receive, 0)
 
     for bz in range(DEPTH // 8):
         for k in range(8 * bz, 8 * bz + 8):
@@ -242,10 +317,15 @@
     blocks = jnp.concatenate(tiles, axis=1)
     high = blocks.astype(BF16)
     low = (blocks - high.astype(F32)).astype(BF16)
-    number = lax.broadcasted_iota(jnp.int32, (HALF, 64), 0)
-    slot = lax.broadcasted_iota(jnp.int32, (HALF, 64), 1)
-    chosen = (number == ids_ref[...]) & (slot < cnt_ref[0, 0])
-    chosen = jnp.where(chosen, 1.0, 0.0).T.astype(BF16)
+    row = lax.broadcasted_iota(jnp.int32, (8, HALF), 0)
+    picks = []
+    for first in range(0, 64, 8):
+        number = jnp.full((8, HALF), -1, jnp.int32)
+        for slot in range(8):
+            live = jnp.where(first + slot < cnt_ref[0, 0], ids_ref[0, first + slot], -1)
+            number = jnp.where(row == slot, live, number)
+        picks.append(jnp.where(number == lane, 1.0, 0.0))
+    chosen = jnp.concatenate(picks, axis=0).astype(BF16)
     high = jnp.dot(chosen, high, preferred_element_type=F32).astype(BF16)
     low = jnp.dot(chosen, low, preferred_element_type=F32).astype(BF16)
     co_ref[...] = (
@@ -254,14 +334,11 @@
         + jnp.dot(high, k_ref[1], preferred_element_type=F32)
     )
 
-    pltpu.make_async_remote_copy(
-        src_ref=plane.at[pl.ds(0, N_SEC - 1)],
-        dst_ref=stacked.at[pl.ds(0, N_SEC - 1)],
-        send_sem=send_sem,
-        recv_sem=recv_sem.at[0],
-        device_id=(peer(0), band),
-        device_id_type=MESH,
-    ).wait_send()
+    sent(send_sem, NY * GROUP_Z - 1)
+
+    @pl.when(jnp.logical_not(late))
+    def _():
+        sent(send_sem, NY * GROUP_Z)
 
     @pl.when(band > 0)
     def _():
@@ -275,6 +352,7 @@
 def on_device(volume, block_ids, counts):
     section = volume.reshape(COLS, ROWS)
     vmem = pl.BlockSpec(memory_space=pltpu.VMEM)
+    smem = pl.BlockSpec(memory_space=pltpu.SMEM)
     hbm = pl.BlockSpec(memory_space=pl.ANY)
     downsampled, coeffs = pl.pallas_call(
         kernel,
@@ -282,7 +360,7 @@
             jax.ShapeDtypeStruct((DEPTH, OUT_COLS, HALF), F32),
             jax.ShapeDtypeStruct((64, 512), F32),
         ),
-        in_specs=[hbm, vmem, pl.BlockSpec(memory_space=pltpu.SMEM), hbm],
+        in_specs=[hbm, smem, smem, hbm],
         out_specs=(vmem, vmem),
         scratch_shapes=[
             pltpu.VMEM((2, COLS + 2 * PAD, HALF), F32),
@@ -299,9 +377,12 @@
             pltpu.SemaphoreType.DMA((N_SEC,)),
             pltpu.SemaphoreType.DMA((2,)),
             pltpu.SemaphoreType.DMA((2,)),
+            pltpu.SemaphoreType.REGULAR,
+            pltpu.SemaphoreType.DMA((GROUP_Z,)),
+            pltpu.SemaphoreType.DMA((GROUP_Z,)),
         ],
         compiler_params=pltpu.CompilerParams(
-            collective_id=0, has_side_effects=True, vmem_limit_bytes=60 * 1024 * 1024
+            collective_id=0, has_side_effects=True, vmem_limit_bytes=53 * 1024 * 1024
         ),
     )(section, block_ids.reshape(1, 64), counts, jnp.asarray(cosine_matrix()))
     return downsampled, coeffs.reshape(1, 1, 64, 512)

time: 52 us -> 49.8 us (0.958)
  local copies, waits for them, and re-layouts: 3.24 us -> 2.01 us
  Pallas kernels: 47.3 us -> 46.4 us
    unnamed x2 -> x4, local copies, waits for them, and re-layouts: 3.24 us -> 2.01 us
    pallas_call x1, Pallas kernels: 47.3 us -> 46.4 us  [on_device(): pl.pallas_call(kernel, out_shape=(jax.ShapeDtypeStruct((DEPTH, OUT_COLS,...]
where the time goes in v2:
time: 49.8 us; the launch traced here: 49.7 us
  Pallas kernels  46.4 us (93%)
  local copies, waits for them, and re-layouts  2.01 us (4%)
  between operations  1.29 us (3%)
    pallas_call x1, Pallas kernels, on_device(): pl.pallas_call(kernel, out_shape=(jax.ShapeDtypeStruct((DEPTH, OUT_COLS,...  46.4 us
    unnamed x4, local copies, waits for them, and re-layouts  2.01 us

profile of v2, /device:TPU:1, one launch (start us, length us, event | category | flops | bytes accessed | tf_op | source)
XLA Modules:
  0.0 49.7 jit_solution(5704986745624844698)
XLA Ops:
  1.3 0.0 copy-start
  1.3 0.6 %copy-done = s32[1,1,64]{2,1,0:T(1,128)S(1)} copy-done((s32[1,1,64]{2,1,0:T(1,128)S(1)}, s32[1,1,64]{2,1,0:T(1,128)}, u32[]{:S(2)}) %copy-start) | copy-done | bytes 280
  1.9 46.4 %shard_map.59 = (f32[32,16,128]{2,1,0:T(8,128)S(1)}, f32[64,512]{1,0:T(8,128)S(1)}) custom-call(f32[2048,256]{1,0:T(8,128)} %bitcast.5, s32[1,64]{1,0:T(1,128)S(1)} %bitcast.4, s32[1,1]{1,0:T(1,128)S(6)} %copy.8.cnt_ref, f32[512,512]{1,0:T(8,128)} %constant.2.clone.k_hbm), custom_call_target="tpu_custom_call" | custom-call | tf_op jit(solution)/shard_map/pallas_call | solution.py:357
  48.3 0.7 %copy.9 = f32[32,16,128]{2,1,0:T(8,128)} copy(f32[32,16,128]{2,1,0:T(8,128)S(1)} %get-tuple-element.8) | data formatting | bytes 524288
  49.0 0.7 %copy.10 = f32[1,1,64,512]{3,2,1,0:T(8,128)} copy(f32[1,1,64,512]{3,2,1,0:T(8,128)S(1)} %bitcast.3) | data formatting | bytes 262144
Async XLA Ops:
  1.3 0.7 %copy-start = (s32[1,1,64]{2,1,0:T(1,128)S(1)}, s32[1,1,64]{2,1,0:T(1,128)}, u32[]{:S(2)}) copy-start(s32[1,1,64]{2,1,0:T(1,128)} %param.5) | copy-start | bytes 772

commit v3 on v2

--- a/solution.py
+++ b/solution.py
@@ -3,7 +3,6 @@
 
 import jax
 import jax.numpy as jnp
-import numpy as np
 from jax import lax
 from jax.experimental import pallas as pl
 from jax.experimental.pallas import tpu as pltpu
@@ -28,11 +27,31 @@
 OWN_ROUNDS = 4
 
 
-def cosine_matrix():
-    index = np.arange(8, dtype=np.float64)
-    weight = np.where(index == 0, math.sqrt(1.0 / 8.0), math.sqrt(2.0 / 8.0))
-    basis = weight[:, None] * np.cos(math.pi * (2.0 * index[None, :] + 1.0) * index[:, None] / 16.0)
-    return np.einsum("ua,vb,wc->cabuvw", basis, basis, basis).reshape(512, 512).astype(np.float32)
+def cosines(frequency, place):
+    turn = ((2 * place + 1) * frequency) % 32
+    value = jnp.zeros(turn.shape, F32)
+    for step in range(32):
+        value = jnp.where(turn == step, math.cos(math.pi * step / 16.0), value)
+    return value * jnp.where(frequency == 0, math.sqrt(1.0 / 8.0), math.sqrt(2.0 / 8.0))
+
+
+def fill_basis(k_ref):
+    place = lax.broadcasted_iota(jnp.int32, (8, 512), 0)
+    output = lax.broadcasted_iota(jnp.int32, (8, 512), 1)
+    along_depth = cosines(output // 64, place)
+    along_column = cosines(output // 8 % 8, place)
+    along_row = cosines(output % 8, place)
+    for c in range(8):
+        for a in range(0, 8, 2):
+            parts = [
+                along_column * (along_row[c : c + 1, :] * along_depth[a + i : a + i + 1, :])
+                for i in range(2)
+            ]
+            value = jnp.concatenate(parts, axis=0)
+            high = value.astype(BF16)
+            rows = pl.ds(64 * c + 8 * a, 16)
+            k_ref[0, rows, :] = high
+            k_ref[1, rows, :] = (value - high.astype(F32)).astype(BF16)
 
 
 def row_matrix(half):
@@ -50,10 +69,10 @@
     return high, mid, (rest - mid.astype(F32)).astype(BF16)
 
 
-def kernel(
-    x_hbm, ids_ref, cnt_ref, k_hbm, ds_ref, co_ref,
-    xbuf, plane, stacked, k_full, k_ref, turned, edge_out, edge_in,
-    x_sem, k_sem, send_sem, recv_sem, edge_send, edge_recv, late_sem, up_sem, down_sem,
+def exchange(
+    x_hbm, stacked, k_ref,
+    xbuf, plane, edge_out, edge_in,
+    x_sem, send_sem, recv_sem, edge_send, edge_recv, late_sem, up_sem, down_sem,
 ):
     me = lax.axis_index("sec")
     band = lax.axis_index("yb")
@@ -72,8 +91,6 @@
     for chunk in range(CHUNKS):
         for half in range(2):
             load(chunk, half).start()
-    basis_copy = pltpu.make_async_copy(k_hbm, k_full, k_sem)
-    basis_copy.start()
 
     late = z >= GROUP_Z
 
@@ -279,9 +296,7 @@
         signal(late_sem, me + GROUP_Z, band)
         visit_group(send, False)
 
-    basis_copy.wait()
-    k_ref[0] = k_full[...].astype(BF16)
-    k_ref[1] = (k_full[...] - k_ref[0].astype(F32)).astype(BF16)
+    fill_basis(k_ref)
 
     def receive(step, carry):
         origin = (me + step) % N_SEC
@@ -290,6 +305,22 @@
 
     lax.fori_loop(1, N_SEC, receive, 0)
 
+    sent(send_sem, NY * GROUP_Z - 1)
+
+    @pl.when(jnp.logical_not(late))
+    def _():
+        sent(send_sem, NY * GROUP_Z)
+
+    @pl.when(band > 0)
+    def _():
+        edge_copy(0, band - 1).wait_send()
+
+    @pl.when(band < N_YB - 1)
+    def _():
+        edge_copy(1, band + 1).wait_send()
+
+
+def transform(stacked, k_ref, ids_ref, cnt_ref, ds_ref, co_ref, turned):
     for bz in range(DEPTH // 8):
         for k in range(8 * bz, 8 * bz + 8):
             value = 3.0 * (stacked[2 * k] + stacked[2 * k + 1])
@@ -304,6 +335,7 @@
         )
         turned[bz] = flat.T
 
+    lane = lax.broadcasted_iota(jnp.int32, (8, HALF), 1)
     wide = lax.broadcasted_iota(jnp.int32, (16, HALF), 1)
     tiles = []
     for pair in range(4):
@@ -334,45 +366,26 @@
         + jnp.dot(high, k_ref[1], preferred_element_type=F32)
     )
 
-    sent(send_sem, NY * GROUP_Z - 1)
-
-    @pl.when(jnp.logical_not(late))
-    def _():
-        sent(send_sem, NY * GROUP_Z)
-
-    @pl.when(band > 0)
-    def _():
-        edge_copy(0, band - 1).wait_send()
-
-    @pl.when(band < N_YB - 1)
-    def _():
-        edge_copy(1, band + 1).wait_send()
-
 
 def on_device(volume, block_ids, counts):
     section = volume.reshape(COLS, ROWS)
     vmem = pl.BlockSpec(memory_space=pltpu.VMEM)
     smem = pl.BlockSpec(memory_space=pltpu.SMEM)
     hbm = pl.BlockSpec(memory_space=pl.ANY)
-    downsampled, coeffs = pl.pallas_call(
-        kernel,
+    stacked, basis = pl.pallas_call(
+        exchange,
         out_shape=(
-            jax.ShapeDtypeStruct((DEPTH, OUT_COLS, HALF), F32),
-            jax.ShapeDtypeStruct((64, 512), F32),
+            jax.ShapeDtypeStruct((N_SEC, OUT_COLS, HALF), F32),
+            jax.ShapeDtypeStruct((2, 512, 512), BF16),
         ),
-        in_specs=[hbm, smem, smem, hbm],
+        in_specs=[hbm],
         out_specs=(vmem, vmem),
         scratch_shapes=[
             pltpu.VMEM((2, COLS + 2 * PAD, HALF), F32),
             pltpu.VMEM((N_SEC, OUT_COLS, HALF), F32),
-            pltpu.VMEM((N_SEC, OUT_COLS, HALF), F32),
-            pltpu.VMEM((512, 512), F32),
-            pltpu.VMEM((2, 512, 512), BF16),
-            pltpu.VMEM((4, HALF, HALF), F32),
             pltpu.VMEM((2, 8, HALF), F32),
             pltpu.VMEM((2, 8, HALF), F32),
             pltpu.SemaphoreType.DMA((CHUNKS, 2)),
-            pltpu.SemaphoreType.DMA,
             pltpu.SemaphoreType.DMA,
             pltpu.SemaphoreType.DMA((N_SEC,)),
             pltpu.SemaphoreType.DMA((2,)),
@@ -382,9 +395,20 @@
             pltpu.SemaphoreType.DMA((GROUP_Z,)),
         ],
         compiler_params=pltpu.CompilerParams(
-            collective_id=0, has_side_effects=True, vmem_limit_bytes=53 * 1024 * 1024
+            collective_id=0, has_side_effects=True, vmem_limit_bytes=207 * 256 * 1024
         ),
-    )(section, block_ids.reshape(1, 64), counts, jnp.asarray(cosine_matrix()))
+    )(section)
+    downsampled, coeffs = pl.pallas_call(
+        transform,
+        out_shape=(
+            jax.ShapeDtypeStruct((DEPTH, OUT_COLS, HALF), F32),
+            jax.ShapeDtypeStruct((64, 512), F32),
+        ),
+        in_specs=[vmem, vmem, smem, smem],
+        out_specs=(vmem, vmem),
+        scratch_shapes=[pltpu.VMEM((4, HALF, HALF), F32)],
+        compiler_params=pltpu.CompilerParams(vmem_limit_bytes=16 * 1024 * 1024),
+    )(stacked, basis, block_ids.reshape(1, 64), counts)
     return downsampled, coeffs.reshape(1, 1, 64, 512)
 
 

time: 49.8 us -> 49.2 us (0.988)
  local copies, waits for them, and re-layouts: 2.01 us -> 0.01 us
  Pallas kernels: 46.4 us -> 47.8 us
    unnamed x4 -> x2, local copies, waits for them, and re-layouts: 2.01 us -> 0.01 us
    pallas_call x1 -> x2, Pallas kernels: 46.4 us -> 47.8 us  [the longest x1 45.9 us: on_device(): pl.pallas_call(exchange, out_shape=(jax.ShapeDtypeStruct((N_SEC, OUT_COLS...]
where the time goes in v3:
time: 49.2 us; the launch traced here: 49.1 us
  Pallas kernels  47.8 us (97%)
  between operations  1.31 us (3%)
    pallas_call x1, Pallas kernels, on_device(): pl.pallas_call(exchange, out_shape=(jax.ShapeDtypeStruct((N_SEC, OUT_COLS...  45.9 us
    pallas_call x1, Pallas kernels, on_device(): pl.pallas_call(transform, out_shape=(jax.ShapeDtypeStruct((DEPTH, OUT_COL...  1.94 us

profile of v3, /device:TPU:1, one launch (start us, length us, event | category | flops | bytes accessed | tf_op | source)
XLA Modules:
  0.0 49.1 jit_solution(883748561826950575)
XLA Ops:
  0.6 0.0 copy-start
  1.3 45.9 %shard_map.50 = (f32[64,16,128]{2,1,0:T(8,128)S(1)}, bf16[2,512,512]{2,1,0:T(8,128)(2,1)S(1)}) custom-call(f32[2048,256]{1,0:T(8,128)} %bitcast.4), custom_call_target="tpu_custom_call" | custom-call | tf_op jit(solution)/shard_map/pallas_call | solution.py:375
  47.2 0.0 copy-done
  47.2 1.9 %shard_map.51 = (f32[32,16,128]{2,1,0:T(8,128)}, f32[64,512]{1,0:T(8,128)}) custom-call(f32[64,16,128]{2,1,0:T(8,128)S(1)} %get-tuple-element.6.stacked, bf16[2,512,512]{2,1,0:T(8,128)(2,1)S(1)} %get-tuple-element.7.k_ref, s32[1,64]{1,0:T(1,128)S(1)} %bitcast.3, s32[1,1]{1,0:T(1,128)S(6)} %copy.5.cnt_ref), custom_call_target="tpu_custom_call" | custom-call | tf_op jit(solution)/shard_map/pallas_call | solution.py:401
Async XLA Ops:
  0.6 46.5 %copy-start = (s32[1,1,64]{2,1,0:T(1,128)S(1)}, s32[1,1,64]{2,1,0:T(1,128)}, u32[]{:S(2)}) copy-start(s32[1,1,64]{2,1,0:T(1,128)} %param.4) | copy-start | bytes 772

commit v4 on v3

--- a/solution.py
+++ b/solution.py
@@ -23,7 +23,6 @@
 PAD = 8
 GROUP_Z = NZ // 2
 WINDOW = 2
-OWN_ROUND = 3
 OWN_ROUNDS = 4
 
 
@@ -238,6 +237,7 @@
         ).wait_send()
 
     place = z - GROUP_Z
+    own_round = 1 + 2 * (band % 2)
 
     def sent_round(index):
         @pl.when(index < place)
@@ -264,14 +264,14 @@
             def _():
                 chunk_copy(column + place + index, me, down_sem.at[index]).start()
 
-        @pl.when(index == OWN_ROUND)
+        @pl.when(index == own_round)
         def _():
             pl.semaphore_wait(late_sem, 1)
 
-        @pl.when((index >= OWN_ROUND) & (index < OWN_ROUND + OWN_ROUNDS))
+        @pl.when((index >= own_round) & (index < own_round + OWN_ROUNDS))
         def _():
             for half in range(GROUP_Z // OWN_ROUNDS):
-                turn = (index - OWN_ROUND) * (GROUP_Z // OWN_ROUNDS) + half
+                turn = (index - own_round) * (GROUP_Z // OWN_ROUNDS) + half
                 target = GROUP_Z + (place + turn) % GROUP_Z
 
                 @pl.when(turn > 0)
@@ -360,10 +360,11 @@
     chosen = jnp.concatenate(picks, axis=0).astype(BF16)
     high = jnp.dot(chosen, high, preferred_element_type=F32).astype(BF16)
     low = jnp.dot(chosen, low, preferred_element_type=F32).astype(BF16)
-    co_ref[...] = (
-        jnp.dot(high, k_ref[0], preferred_element_type=F32)
-        + jnp.dot(low, k_ref[0], preferred_element_type=F32)
-        + jnp.dot(high, k_ref[1], preferred_element_type=F32)
+    both = jnp.dot(
+        jnp.concatenate([high, low], axis=0), k_ref[0], preferred_element_type=F32
+    )
+    co_ref[...] = both[0:64] + both[64:128] + jnp.dot(
+        high, k_ref[1], preferred_element_type=F32
     )
 
 

time: 49.2 us -> 49.1 us (level)
  no operation moved by 1% of the time
where the time goes in v4:
time: 49.1 us; the launch traced here: 49 us
  Pallas kernels  47.7 us (97%)
  between operations  1.31 us (3%)
    pallas_call x1, Pallas kernels, on_device(): pl.pallas_call(exchange, out_shape=(jax.ShapeDtypeStruct((N_SEC, OUT_COLS...  45.9 us
    pallas_call x1, Pallas kernels, on_device(): pl.pallas_call(transform, out_shape=(jax.ShapeDtypeStruct((DEPTH, OUT_COL...  1.83 us

profile of v4, /device:TPU:1, one launch (start us, length us, event | category | flops | bytes accessed | tf_op | source)
XLA Modules:
  0.0 49.0 jit_solution(16411646819216416712)
XLA Ops:
  0.6 0.0 copy-start
  1.3 45.9 %shard_map.50 = (f32[64,16,128]{2,1,0:T(8,128)S(1)}, bf16[2,512,512]{2,1,0:T(8,128)(2,1)S(1)}) custom-call(f32[2048,256]{1,0:T(8,128)} %bitcast.4), custom_call_target="tpu_custom_call" | custom-call | tf_op jit(solution)/shard_map/pallas_call | solution.py:376
  47.2 0.0 copy-done
  47.2 1.8 %shard_map.51 = (f32[32,16,128]{2,1,0:T(8,128)}, f32[64,512]{1,0:T(8,128)}) custom-call(f32[64,16,128]{2,1,0:T(8,128)S(1)} %get-tuple-element.6.stacked, bf16[2,512,512]{2,1,0:T(8,128)(2,1)S(1)} %get-tuple-element.7.k_ref, s32[1,64]{1,0:T(1,128)S(1)} %bitcast.3, s32[1,1]{1,0:T(1,128)S(6)} %copy.5.cnt_ref), custom_call_target="tpu_custom_call" | custom-call | tf_op jit(solution)/shard_map/pallas_call | solution.py:402
Async XLA Ops:
  0.6 46.5 %copy-start = (s32[1,1,64]{2,1,0:T(1,128)S(1)}, s32[1,1,64]{2,1,0:T(1,128)}, u32[]{:S(2)}) copy-start(s32[1,1,64]{2,1,0:T(1,128)} %param.4) | copy-start | bytes 772

commit v5 on v4

--- a/solution.py
+++ b/solution.py
@@ -216,7 +216,7 @@
             src_ref=plane.at[target],
             dst_ref=stacked.at[slot],
             send_sem=semaphore,
-            recv_sem=recv_sem.at[slot],
+            recv_sem=recv_sem,
             device_id=(target, band),
             device_id_type=MESH,
         )
@@ -231,7 +231,7 @@
             src_ref=plane.at[pl.ds(0, count)],
             dst_ref=stacked.at[pl.ds(0, count)],
             send_sem=semaphore,
-            recv_sem=recv_sem.at[0],
+            recv_sem=recv_sem,
             device_id=((me + 1) % N_SEC, band),
             device_id_type=MESH,
         ).wait_send()
@@ -298,12 +298,14 @@
 
     fill_basis(k_ref)
 
-    def receive(step, carry):
-        origin = (me + step) % N_SEC
-        chunk_copy(origin, origin).wait_recv()
-        return carry
-
-    lax.fori_loop(1, N_SEC, receive, 0)
+    pltpu.make_async_remote_copy(
+        src_ref=plane.at[pl.ds(0, N_SEC - 1)],
+        dst_ref=stacked.at[pl.ds(0, N_SEC - 1)],
+        send_sem=send_sem,
+        recv_sem=recv_sem,
+        device_id=((me + 1) % N_SEC, band),
+        device_id_type=MESH,
+    ).wait_recv()
 
     sent(send_sem, NY * GROUP_Z - 1)
 
@@ -388,7 +390,7 @@
             pltpu.VMEM((2, 8, HALF), F32),
             pltpu.SemaphoreType.DMA((CHUNKS, 2)),
             pltpu.SemaphoreType.DMA,
-            pltpu.SemaphoreType.DMA((N_SEC,)),
+            pltpu.SemaphoreType.DMA,
             pltpu.SemaphoreType.DMA((2,)),
             pltpu.SemaphoreType.DMA((2,)),
             pltpu.SemaphoreType.REGULAR,

time: 49.1 us -> 48.6 us (0.990)
  Pallas kernels: 47.7 us -> 47.1 us
    pallas_call x1, Pallas kernels: 45.9 us -> 45.3 us  [on_device(): pl.pallas_call(exchange, out_shape=(jax.ShapeDtypeStruct((N_SEC, OUT_COLS...]
where the time goes in v5:
time: 48.6 us; the launch traced here: 48.4 us
  Pallas kernels  47.1 us (97%)
  between operations  1.31 us (3%)
    pallas_call x1, Pallas kernels, on_device(): pl.pallas_call(exchange, out_shape=(jax.ShapeDtypeStruct((N_SEC, OUT_COLS...  45.3 us
    pallas_call x1, Pallas kernels, on_device(): pl.pallas_call(transform, out_shape=(jax.ShapeDtypeStruct((DEPTH, OUT_COL...  1.82 us

profile of v5, /device:TPU:1, one launch (start us, length us, event | category | flops | bytes accessed | tf_op | source)
XLA Modules:
  0.0 48.4 jit_solution(4552169384163549315)
XLA Ops:
  0.6 0.0 copy-start
  1.3 45.3 %shard_map.50 = (f32[64,16,128]{2,1,0:T(8,128)S(1)}, bf16[2,512,512]{2,1,0:T(8,128)(2,1)S(1)}) custom-call(f32[2048,256]{1,0:T(8,128)} %bitcast.4), custom_call_target="tpu_custom_call" | custom-call | tf_op jit(solution)/shard_map/pallas_call | solution.py:378
  46.6 0.0 copy-done
  46.6 1.8 %shard_map.51 = (f32[32,16,128]{2,1,0:T(8,128)}, f32[64,512]{1,0:T(8,128)}) custom-call(f32[64,16,128]{2,1,0:T(8,128)S(1)} %get-tuple-element.6.stacked, bf16[2,512,512]{2,1,0:T(8,128)(2,1)S(1)} %get-tuple-element.7.k_ref, s32[1,64]{1,0:T(1,128)S(1)} %bitcast.3, s32[1,1]{1,0:T(1,128)S(6)} %copy.5.cnt_ref), custom_call_target="tpu_custom_call" | custom-call | tf_op jit(solution)/shard_map/pallas_call | solution.py:404
Async XLA Ops:
  0.6 46.0 %copy-start = (s32[1,1,64]{2,1,0:T(1,128)S(1)}, s32[1,1,64]{2,1,0:T(1,128)}, u32[]{:S(2)}) copy-start(s32[1,1,64]{2,1,0:T(1,128)} %param.4) | copy-start | bytes 772

commit v6 on v5

--- a/solution.py
+++ b/solution.py
@@ -298,6 +298,20 @@
 
     fill_basis(k_ref)
 
+    sent(send_sem, NY * GROUP_Z - 1)
+
+    @pl.when(jnp.logical_not(late))
+    def _():
+        sent(send_sem, NY * GROUP_Z)
+
+    @pl.when(band > 0)
+    def _():
+        edge_copy(0, band - 1).wait_send()
+
+    @pl.when(band < N_YB - 1)
+    def _():
+        edge_copy(1, band + 1).wait_send()
+
     pltpu.make_async_remote_copy(
         src_ref=plane.at[pl.ds(0, N_SEC - 1)],
         dst_ref=stacked.at[pl.ds(0, N_SEC - 1)],
@@ -306,20 +320,6 @@
         device_id=((me + 1) % N_SEC, band),
         device_id_type=MESH,
     ).wait_recv()
-
-    sent(send_sem, NY * GROUP_Z - 1)
-
-    @pl.when(jnp.logical_not(late))
-    def _():
-        sent(send_sem, NY * GROUP_Z)
-
-    @pl.when(band > 0)
-    def _():
-        edge_copy(0, band - 1).wait_send()
-
-    @pl.when(band < N_YB - 1)
-    def _():
-        edge_copy(1, band + 1).wait_send()
 
 
 def transform(stacked, k_ref, ids_ref, cnt_ref, ds_ref, co_ref, turned):

time: 48.6 us -> 48.6 us (level)
  no operation moved by 1% of the time
where the time goes in v6:
time: 48.6 us; the launch traced here: 48.4 us
  Pallas kernels  47.1 us (97%)
  between operations  1.31 us (3%)
    pallas_call x1, Pallas kernels, on_device(): pl.pallas_call(exchange, out_shape=(jax.ShapeDtypeStruct((N_SEC, OUT_COLS...  45.3 us
    pallas_call x1, Pallas kernels, on_device(): pl.pallas_call(transform, out_shape=(jax.ShapeDtypeStruct((DEPTH, OUT_COL...  1.83 us

profile of v6, /device:TPU:1, one launch (start us, length us, event | category | flops | bytes accessed | tf_op | source)
XLA Modules:
  0.0 48.4 jit_solution(14841870762489174441)
XLA Ops:
  0.6 0.0 copy-start
  1.3 45.3 %shard_map.50 = (f32[64,16,128]{2,1,0:T(8,128)S(1)}, bf16[2,512,512]{2,1,0:T(8,128)(2,1)S(1)}) custom-call(f32[2048,256]{1,0:T(8,128)} %bitcast.4), custom_call_target="tpu_custom_call" | custom-call | tf_op jit(solution)/shard_map/pallas_call | solution.py:378
  46.6 0.0 copy-done
  46.6 1.8 %shard_map.51 = (f32[32,16,128]{2,1,0:T(8,128)}, f32[64,512]{1,0:T(8,128)}) custom-call(f32[64,16,128]{2,1,0:T(8,128)S(1)} %get-tuple-element.6.stacked, bf16[2,512,512]{2,1,0:T(8,128)(2,1)S(1)} %get-tuple-element.7.k_ref, s32[1,64]{1,0:T(1,128)S(1)} %bitcast.3, s32[1,1]{1,0:T(1,128)S(6)} %copy.5.cnt_ref), custom_call_target="tpu_custom_call" | custom-call | tf_op jit(solution)/shard_map/pallas_call | solution.py:404
Async XLA Ops:
  0.6 46.0 %copy-start = (s32[1,1,64]{2,1,0:T(1,128)S(1)}, s32[1,1,64]{2,1,0:T(1,128)}, u32[]{:S(2)}) copy-start(s32[1,1,64]{2,1,0:T(1,128)} %param.4) | copy-start | bytes 772
